TPU v7x, 256 devices: a whole 4x4x8 slice. The times are simulated.
256 devices in a mesh: seq: 32 (over x, y, core), ch: 8 (over z).
Axes of the slice: x: 4, y: 4, z: 8, core: 2. Of those that a mesh axis runs over, the one named last changes fastest.
Arguments:
- queries: bfloat16 [4096, 8192], P('seq', 'ch'), may hold values from -6 to 6
- keys: bfloat16 [4096, 8192], P('seq', 'ch'), may hold values from -6 to 6
- values: bfloat16 [4096, 8192], P('seq', 'ch'), may hold values from -6 to 6
- filters: bfloat16 [4096, 8192], P('seq', 'ch'), may hold values from -0.09375 to 0.09375
- short_weight: bfloat16 [3, 7, 8192], P(None, None, 'ch'), may hold values from -2 to 2
- skip_gain: float32 [8192], P('ch'), may hold values from -4 to 4
- residual: bfloat16 [4096, 8192], P('seq', 'ch'), may hold values from -30 to 30
- norm_gain: float32 [8192], P('ch'), may hold values from 0.5 to 1.5
Outputs:
- stream_out: bfloat16 [4096, 8192], P('seq', 'ch')
- normed: bfloat16 [4096, 8192], P('seq', 'ch')
All inputs are finite; a program needn't handle non-finite values.
Results may differ from a plain program's by a relative error of at most 0.0065.
Values may be sent and summed in bfloat16 or wider, within the bound.
A program may use at most 64 MiB of HBM per device.

v0:
```python
import functools
import math

import jax
import jax.numpy as jnp
import numpy as np
from jax import lax
from jax.experimental import pallas as pl
from jax.experimental.pallas import tpu as pltpu
from jax.sharding import PartitionSpec as P

F32 = jnp.float32
BF16 = jnp.bfloat16
LANES = 128
GROUP = 16
PARTS = 32
ROOT = math.sqrt(0.5)

KEPT = (
    [0, 8, 16, 24, 32]
    + [1 + 8 * b for b in range(8)]
    + [2 + 8 * b for b in range(8)]
    + [3 + 8 * b for b in range(8)]
    + [4 + 8 * b for b in range(4)]
)
PLACE = {k1: i for i, k1 in enumerate(KEPT)}
ROWS = len(KEPT) * GROUP
CHUNK = 11 * GROUP


def tables():
    lane = np.arange(LANES)
    angle = 2.0 * np.pi * (np.outer(lane, lane) % LANES) / LANES
    cos, sin = np.cos(angle), np.sin(angle)
    forward = np.block([[cos, -sin], [sin, cos]])
    backward = np.block([[cos, sin], [-sin, cos]])
    parts = []
    for matrix in (forward, backward):
        high = matrix.astype(np.float32).astype(jnp.bfloat16)
        low = (matrix - high.astype(np.float64)).astype(np.float32).astype(jnp.bfloat16)
        parts += [high, low]
    matrices = np.stack(parts)
    turn = 2.0 * np.pi * np.outer(KEPT, lane) / (64 * LANES)
    weight = np.where(np.isin(KEPT, [0, 32]), 1.0, 2.0)[:, None] / (64 * LANES)
    twist = np.stack([np.cos(turn), -np.sin(turn), weight * np.cos(turn), weight * np.sin(turn)])
    return matrices, twist.astype(np.float32)


def plus(a, b):
    if a is None:
        return b
    return a if b is None else a + b


def neg(a):
    return None if a is None else -a


def minus(a, b):
    if b is None:
        return a
    return -b if a is None else a - b


def scaled(a, factor):
    return None if a is None else a * factor


def cplus(a, b):
    return (plus(a[0], b[0]), plus(a[1], b[1]))


def cminus(a, b):
    return (minus(a[0], b[0]), minus(a[1], b[1]))


def quarter(a, sign):
    return (neg(a[1]), a[0]) if sign > 0 else (a[1], neg(a[0]))


def turned(a, angle):
    cos, sin = math.cos(angle), math.sin(angle)
    if angle == 0.0:
        return a
    return (
        minus(scaled(a[0], cos), scaled(a[1], sin)),
        plus(scaled(a[1], cos), scaled(a[0], sin)),
    )


def dft4(z, sign):
    a, b = cplus(z[0], z[2]), cminus(z[0], z[2])
    c, d = cplus(z[1], z[3]), quarter(cminus(z[1], z[3]), sign)
    return [cplus(a, c), cplus(b, d), cminus(a, c), cminus(b, d)]


def dft8(z, sign):
    even, odd = dft4(z[0::2], sign), dft4(z[1::2], sign)
    a, b = odd[1], odd[3]
    if sign > 0:
        first = (scaled(minus(a[0], a[1]), ROOT), scaled(plus(a[0], a[1]), ROOT))
        third = (scaled(plus(b[0], b[1]), -ROOT), scaled(minus(b[0], b[1]), ROOT))
    else:
        first = (scaled(plus(a[0], a[1]), ROOT), scaled(minus(a[1], a[0]), ROOT))
        third = (scaled(minus(b[1], b[0]), ROOT), scaled(plus(b[0], b[1]), -ROOT))
    odd = [odd[0], first, quarter(odd[2], sign), third]
    return [cplus(e, o) for e, o in zip(even, odd)] + [cminus(e, o) for e, o in zip(even, odd)]


def forward64(x):
    column = [[None] * 8 for _ in range(5)]
    for s in range(8):
        x0, x1, x2, x3 = x[s], x[8 + s], x[16 + s], x[24 + s]
        a, b, c, d = x0 + x2, x1 + x3, x0 - x2, (x1 - x3)
        rb, rd = b * ROOT, d * ROOT
        values = [(a + b, None), (x0 + rd, -x2 - rb), (c, -d), (x0 - rd, x2 - rb), (a - b, None)]
        for k in range(5):
            column[k][s] = turned(values[k], -2.0 * math.pi * s * k / 64)
    out = {}
    for k in range(5):
        result = dft8(column[k], -1)
        for b in range((5, 8, 8, 8, 4)[k]):
            out[k + 8 * b] = result[b]
    return out


def backward64(get):
    v = []
    for k in range(5):
        count = (5, 8, 8, 8, 4)[k]
        z = [get(k + 8 * b) if b < count else (None, None) for b in range(8)]
        if k == 0:
            z[0], z[4] = (z[0][0], None), (z[4][0], None)
        u = dft8(z, 1)
        v.append([turned(u[s], 2.0 * math.pi * s * k / 64) for s in range(8)])
    y = [None] * 32
    for s in range(8):
        (a, _), (br, bi), (cr, ci), (dr, di), (e, _) = [v[k][s] for k in range(5)]
        p, m = a + e, a - e
        y[s] = (p + cr) + (br + dr)
        y[16 + s] = (p - cr) + (di - bi)
        f, g = (br - dr) * ROOT, (bi + di) * ROOT
        y[8 + s] = (m - ci) + (f - g)
        y[24 + s] = (m + ci) - (f + g)
    return y


def split(a):
    high = a.astype(BF16)
    return high, (a - high.astype(F32)).astype(BF16)


def product3(high, low, matrix_high, matrix_low):
    dot = functools.partial(jnp.dot, preferred_element_type=F32)
    return dot(high, matrix_high) + (dot(low, matrix_high) + dot(high, matrix_low))


def kernel(
    queries, keys, values, filters, short_taps, skip, residual, gain, matrices, twist,
    stream_out, normed,
    q_in, k_in, v_in, f_in, r_in, short_weight, skip_gain, norm_gain, mat, tw, halo, ext, mixed, short_q, base, stream_f, out_bf, norm_bf,
    send_f, send_m, got_f, got_m, send_y, got_y, a_high, a_low, spec_f, back, sums, own_sum,
    in_sem, halo_send, halo_recv, f_send, f_recv, m_send, m_recv, y_send, y_recv, p_send, p_recv, out_sem,
):
    parts, rounds = lax.axis_size("seq"), lax.axis_size("ch")
    me, plane = lax.axis_index("seq"), lax.axis_index("ch")
    rows, width = q_in.shape
    own = width // parts
    halves = own // GROUP
    blocks = width // LANES

    barrier = pltpu.get_barrier_semaphore()

    @pl.loop(1, parts)
    def _(d):
        pl.semaphore_signal(barrier, inc=1, device_id={"seq": lax.rem(me + d, parts)})

    @pl.loop(1, rounds)
    def _(d):
        pl.semaphore_signal(barrier, inc=1, device_id={"ch": lax.rem(plane + d, rounds)})

    loads = [
        pltpu.make_async_copy(source, target, in_sem.at[i])
        for i, (source, target) in enumerate(
            [
                (filters, f_in), (keys, k_in), (values, v_in), (queries, q_in), (residual, r_in),
                (short_taps, short_weight), (skip, skip_gain), (gain, norm_gain),
                (matrices, mat), (twist, tw),
            ]
        )
    ]
    for load in loads:
        load.start()

    def lanes(b):
        return pl.ds(pl.multiple_of(b * LANES, LANES), LANES)

    loads[0].wait()

    @pl.loop(0, blocks)
    def _(b):
        send_f[lanes(b), :] = f_in[:, lanes(b)].astype(F32).T.astype(BF16)

    for i in (1, 2, 3):
        loads[i].wait()
    for i, stream in enumerate((q_in, k_in, v_in)):
        ext[i, pl.ds(8, rows), :] = stream[...].astype(F32)

    pl.semaphore_wait(barrier, parts - 1 + rounds - 1)

    halo_copies = [
        pltpu.make_async_remote_copy(
            src_ref=stream.at[pl.ds(rows - GROUP, GROUP)],
            dst_ref=halo.at[i],
            send_sem=halo_send.at[i],
            recv_sem=halo_recv.at[i],
            device_id={"seq": lax.rem(me + 1, parts)},
        )
        for i, stream in enumerate((q_in, k_in, v_in))
    ]
    for i in (1, 2, 0):
        halo_copies[i].start()

    def own_rows(peer, h):
        return pl.ds(pl.multiple_of(peer * own + h * GROUP, GROUP), GROUP)

    def exchange(source, target, send_sem, recv_sem):
        pltpu.make_async_copy(source(me), target, recv_sem).start()

        @pl.loop(1, parts)
        def _(d):
            peer = lax.rem(me + d, parts)
            pltpu.make_async_remote_copy(
                src_ref=source(peer),
                dst_ref=target,
                send_sem=send_sem,
                recv_sem=recv_sem,
                device_id={"seq": peer},
            ).start()

    for h in range(halves):
        exchange(
            lambda peer: send_f.at[own_rows(peer, h)], got_f.at[h, me], f_send.at[h], f_recv.at[h]
        )

    for i in (1, 2):
        halo_copies[i].wait_recv()
    loads[5].wait()
    first = me == 0
    for i in (1, 2):
        ext[i, pl.ds(0, 8), :] = jnp.where(first, 0.0, halo[i].astype(F32)[8:, :])

    def short(i, b):
        weights = short_weight[i, :, lanes(b)].astype(F32)
        total = weights[0:1] * ext[i, pl.ds(8, rows), lanes(b)]
        for j in range(1, weights.shape[0]):
            total = total + weights[j : j + 1] * ext[i, pl.ds(8 - j, rows), lanes(b)]
        return total

    @pl.loop(0, blocks)
    def _(b):
        product = (short(1, b) * short(2, b)).astype(BF16)
        mixed[:, lanes(b)] = product
        send_m[lanes(b), :] = product.astype(F32).T.astype(BF16)

    for h in range(halves):
        exchange(
            lambda peer: send_m.at[own_rows(peer, h)], got_m.at[h, me], m_send.at[h], m_recv.at[h]
        )

    halo_copies[0].wait_recv()
    ext[0, pl.ds(0, 8), :] = jnp.where(first, 0.0, halo[0].astype(F32)[8:, :])
    loads[4].wait()
    loads[6].wait()

    @pl.loop(0, blocks)
    def _(b):
        gate = short(0, b)
        short_q[:, lanes(b)] = gate
        direct = skip_gain[:, lanes(b)] * mixed[:, lanes(b)].astype(F32)
        base[:, lanes(b)] = r_in[:, lanes(b)].astype(F32) + gate * direct

    loads[8].wait()
    loads[9].wait()

    def twisted(value, i, which):
        cos, sin = tw[which, pl.ds(i, 1), :], tw[which + 1, pl.ds(i, 1), :]
        if value[1] is None:
            return value[0] * cos, value[0] * sin
        return value[0] * cos - value[1] * sin, value[1] * cos + value[0] * sin

    def first_stage(got, h):
        spectrum = forward64([got[h, s].astype(F32) for s in range(PARTS)])
        for k1 in KEPT:
            i = PLACE[k1]
            for half, part in enumerate(twisted(spectrum[k1], i, 0)):
                high, low = split(part)
                place = (pl.ds(i * GROUP, GROUP), pl.ds(half * LANES, LANES))
                a_high[place] = high
                a_low[place] = low

    for h in range(halves):
        pltpu.make_async_copy(got_f.at[h], got_f.at[h], f_recv.at[h]).wait()

    @pl.loop(0, halves)
    def _(h):
        first_stage(got_f, h)
        for c in range(ROWS // CHUNK):
            chunk = pl.ds(c * CHUNK, CHUNK)
            spec_f[h, chunk, :] = product3(a_high[chunk, :], a_low[chunk, :], mat[0], mat[1])

    @pl.loop(0, halves)
    def _(h):
        pltpu.make_async_copy(got_m.at[h], got_m.at[h], m_recv.at[h]).wait()
        first_stage(got_m, h)
        for c in range(ROWS // CHUNK):
            chunk = pl.ds(c * CHUNK, CHUNK)
            signal = product3(a_high[chunk, :], a_low[chunk, :], mat[0], mat[1])
            taps = spec_f[h, chunk, :]
            sr, si = signal[:, :LANES], signal[:, LANES:]
            fr, fi = taps[:, :LANES], taps[:, LANES:]
            both = jnp.concatenate([sr * fr - si * fi, sr * fi + si * fr], axis=1)
            high, low = split(both)
            back[chunk, :] = product3(high, low, mat[2], mat[3])

        def value(k1):
            i = PLACE[k1]
            part = pl.ds(i * GROUP, GROUP)
            return twisted((back[part, pl.ds(0, LANES)], back[part, pl.ds(LANES, LANES)]), i, 2)

        for s, y in enumerate(backward64(value)):
            send_y[h, s] = y.astype(BF16)
        exchange(lambda peer: send_y.at[h, peer], got_y.at[own_rows(me, h)], y_send.at[h], y_recv)

    pltpu.make_async_copy(got_y, got_y, y_recv).wait()

    partial = jnp.zeros((rows, LANES), F32)
    for b in range(blocks):
        at = pl.ds(b * LANES, LANES)
        conv = got_y[at, :].astype(F32).T
        rounded = (base[:, at] + short_q[:, at] * conv).astype(BF16)
        out_bf[:, at] = rounded
        value = rounded.astype(F32)
        stream_f[:, at] = value
        partial = partial + value * value
    write_stream = pltpu.make_async_copy(out_bf, stream_out, out_sem.at[0])
    write_stream.start()

    own_sum[...] = jnp.broadcast_to(jnp.sum(partial.T, axis=0, keepdims=True), own_sum.shape)
    pltpu.make_async_copy(own_sum, sums.at[plane], p_recv).start()

    @pl.loop(1, rounds)
    def _(d):
        pltpu.make_async_remote_copy(
            src_ref=own_sum,
            dst_ref=sums.at[plane],
            send_sem=p_send,
            recv_sem=p_recv,
            device_id={"ch": lax.rem(plane + d, rounds)},
        ).start()

    pltpu.make_async_copy(sums, sums, p_recv).wait()
    power = jnp.sum(sums[...], axis=0)[0:1] / (width * rounds)
    loads[7].wait()
    scale = jnp.broadcast_to(lax.rsqrt(power + 1e-05), (LANES, rows)).T
    for b in range(blocks):
        at = pl.ds(b * LANES, LANES)
        norm_bf[:, at] = (stream_f[:, at] * scale * norm_gain[:, at]).astype(BF16)
    write_normed = pltpu.make_async_copy(norm_bf, normed, out_sem.at[1])
    write_normed.start()

    for copy in halo_copies:
        copy.wait_send()
    others = pl.ds(0, parts - 1)
    for h in range(halves):
        pltpu.make_async_copy(got_f.at[h, others], got_f.at[h, others], f_send.at[h]).wait()
        pltpu.make_async_copy(got_m.at[h, others], got_m.at[h, others], m_send.at[h]).wait()
        pltpu.make_async_copy(got_m.at[h, others], got_m.at[h, others], y_send.at[h]).wait()
    if rounds > 1:
        most = sums.at[pl.ds(0, rounds - 1)]
        pltpu.make_async_copy(most, most, p_send).wait()
    write_stream.wait()
    write_normed.wait()


def shards(queries, keys, values, filters, short_weight, skip_gain, residual, norm_gain):
    rows, width = queries.shape
    parts, rounds = lax.axis_size("seq"), lax.axis_size("ch")
    taps = short_weight.shape[1]
    own = width // parts
    halves = own // GROUP
    assert parts == PARTS and rows == LANES and own % GROUP == 0
    matrices, twist = tables()
    block = (rows, width)
    whole = pl.BlockSpec(memory_space=pltpu.HBM)
    dma = pltpu.SemaphoreType.DMA
    return pl.pallas_call(
        kernel,
        out_shape=(jax.ShapeDtypeStruct(block, BF16), jax.ShapeDtypeStruct(block, BF16)),
        in_specs=[whole] * 10,
        out_specs=(whole, whole),
        scratch_shapes=[
            pltpu.VMEM(block, BF16),
            pltpu.VMEM(block, BF16),
            pltpu.VMEM(block, BF16),
            pltpu.VMEM(block, BF16),
            pltpu.VMEM(block, BF16),
            pltpu.VMEM((3, taps, width), BF16),
            pltpu.VMEM((1, width), F32),
            pltpu.VMEM((1, width), F32),
            pltpu.VMEM(matrices.shape, BF16),
            pltpu.VMEM(twist.shape, F32),
            pltpu.VMEM((3, GROUP, width), BF16),
            pltpu.VMEM((3, rows + 8, width), F32),
            pltpu.VMEM(block, BF16),
            pltpu.VMEM(block, F32),
            pltpu.VMEM(block, F32),
            pltpu.VMEM(block, F32),
            pltpu.VMEM(block, BF16),
            pltpu.VMEM(block, BF16),
            pltpu.VMEM((width, rows), BF16),
            pltpu.VMEM((width, rows), BF16),
            pltpu.VMEM((halves, parts, GROUP, LANES), BF16),
            pltpu.VMEM((halves, parts, GROUP, LANES), BF16),
            pltpu.VMEM((halves, parts, GROUP, LANES), BF16),
            pltpu.VMEM((width, rows), BF16),
            pltpu.VMEM((ROWS, 2 * LANES), BF16),
            pltpu.VMEM((ROWS, 2 * LANES), BF16),
            pltpu.VMEM((halves, ROWS, 2 * LANES), F32),
            pltpu.VMEM((ROWS, 2 * LANES), F32),
            pltpu.VMEM((rounds, 8, LANES), F32),
            pltpu.VMEM((8, LANES), F32),
            dma((10,)),
            dma((3,)),
            dma((3,)),
            dma((halves,)),
            dma((halves,)),
            dma((halves,)),
            dma((halves,)),
            dma((halves,)),
            dma,
            dma,
            dma,
            dma((2,)),
        ],
        compiler_params=pltpu.CompilerParams(
            collective_id=0, has_side_effects=True, vmem_limit_bytes=60 * 1024 * 1024
        ),
        cost_estimate=pl.CostEstimate(flops=2 * 10**9, bytes_accessed=2 * 10**6, transcendentals=0),
    )(
        queries, keys, values, filters, short_weight, skip_gain[None, :], residual, norm_gain[None, :],
        jnp.asarray(matrices), jnp.asarray(twist),
    )


def solution(mesh):
    placed = (
        P("seq", "ch"),
        P("seq", "ch"),
        P("seq", "ch"),
        P("seq", "ch"),
        P(None, None, "ch"),
        P("ch"),
        P("seq", "ch"),
        P("ch"),
    )
    return jax.shard_map(
        shards,
        mesh=mesh,
        in_specs=placed,
        out_specs=(P("seq", "ch"), P("seq", "ch")),
        check_vma=False,
    )
```

profile of v0, /device:TPU:1, one launch (start us, length us, event | category | flops | bytes accessed | tf_op | source)
XLA Modules:
  0.0 38.1 jit_solution(14561051661736146825)
XLA Ops:
  0.6 35.0 %shard_map.113 = (bf16[128,1024]{1,0:T(8,128)(2,1)}, bf16[128,1024]{1,0:T(8,128)(2,1)}) custom-call(bf16[128,1024]{1,0:T(8,128)(2,1)} %queries.1, bf16[128,1024]{1,0:T(8,128)(2,1)} %keys.1, bf16[128,1024]{1,0:T(8,128)(2,1)} %values.1, bf16[128,1024]{1,0:T(8,128)(2,1)} %filters.1, bf16[3,7,1024]{2,1,0:T(8,128)(2,1)} %short_taps.1, f32[1,1024]{1,0:T(1,128)} %bitcast.2, ...), custom_call_target="tpu_custom_call" | custom-call | flops 2000000000 | bytes 2000000 | tf_op jit(solution)/shard_map/pallas_call | solution.py:397
  35.7 0.0 copy-start
  35.7 1.7 %copy.14 = bf16[128,1024]{1,0:T(8,128)(2,1)} copy(bf16[128,1024]{1,0:T(8,128)(2,1)} %get-tuple-element.4) | data formatting | bytes 524288
  37.4 0.0 copy-done
  37.4 0.7 %copy.15 = bf16[128,1024]{1,0:T(8,128)(2,1)} copy(bf16[128,1024]{1,0:T(8,128)(2,1)S(1)} %copy-done) | data formatting | bytes 524288
Async XLA Ops:
  35.7 1.7 %copy-start = (bf16[128,1024]{1,0:T(8,128)(2,1)S(1)}, bf16[128,1024]{1,0:T(8,128)(2,1)}, u32[]{:S(2)}) copy-start(bf16[128,1024]{1,0:T(8,128)(2,1)} %get-tuple-element.5) | copy-start | bytes 786436
where the time goes:
time: 38.2 us; the launch traced here: 38.1 us
  Pallas kernels  35 us (92%)
  local copies, waits for them, and re-layouts  2.42 us (6%)
  between operations  0.65 us (2%)
    pallas_call x1, Pallas kernels, shards(): pl.pallas_call(kernel, out_shape=(jax.ShapeDtypeStruct(block, BF16), jax....  35 us
    unnamed x4, local copies, waits for them, and re-layouts  2.42 us

commit v1 on v0

--- a/solution.py
+++ b/solution.py
@@ -26,6 +26,12 @@
 PLACE = {k1: i for i, k1 in enumerate(KEPT)}
 ROWS = len(KEPT) * GROUP
 CHUNK = 11 * GROUP
+
+
+STEPS = sorted(
+    ((dx, dy, dc) for dx in range(4) for dy in range(4) for dc in range(2) if dx + dy + dc > 0),
+    key=lambda step: -(min(step[0], 4 - step[0]) + min(step[1], 4 - step[1])),
+)
 
 
 def tables():
@@ -157,10 +163,10 @@
 
 def kernel(
     queries, keys, values, filters, short_taps, skip, residual, gain, matrices, twist,
-    stream_out, normed,
-    q_in, k_in, v_in, f_in, r_in, short_weight, skip_gain, norm_gain, mat, tw, halo, ext, mixed, short_q, base, stream_f, out_bf, norm_bf,
+    total_f, scale_v, gain_v,
+    q_in, k_in, v_in, f_in, r_in, short_weight, skip_gain, mat, tw, tail_kv, halo, ext, mixed, short_q, base,
     send_f, send_m, got_f, got_m, send_y, got_y, a_high, a_low, spec_f, back, sums, own_sum,
-    in_sem, halo_send, halo_recv, f_send, f_recv, m_send, m_recv, y_send, y_recv, p_send, p_recv, out_sem,
+    in_sem, halo_send, halo_recv, f_send, f_recv, m_send, m_recv, y_send, y_recv, p_send, p_recv,
 ):
     parts, rounds = lax.axis_size("seq"), lax.axis_size("ch")
     me, plane = lax.axis_index("seq"), lax.axis_index("ch")
@@ -184,7 +190,7 @@
         for i, (source, target) in enumerate(
             [
                 (filters, f_in), (keys, k_in), (values, v_in), (queries, q_in), (residual, r_in),
-                (short_taps, short_weight), (skip, skip_gain), (gain, norm_gain),
+                (short_taps, short_weight), (skip, skip_gain), (gain, gain_v),
                 (matrices, mat), (twist, tw),
             ]
         )
@@ -206,30 +212,38 @@
     for i, stream in enumerate((q_in, k_in, v_in)):
         ext[i, pl.ds(8, rows), :] = stream[...].astype(F32)
 
+    last = pl.ds(rows - GROUP, GROUP)
+    tail_kv[...] = jnp.concatenate(
+        [k_in[last, :].astype(F32)[8:], v_in[last, :].astype(F32)[8:]], axis=0
+    ).astype(BF16)
+
     pl.semaphore_wait(barrier, parts - 1 + rounds - 1)
 
-    halo_copies = [
+    after = {"seq": lax.rem(me + 1, parts)}
+    tails = [
         pltpu.make_async_remote_copy(
-            src_ref=stream.at[pl.ds(rows - GROUP, GROUP)],
+            src_ref=source,
             dst_ref=halo.at[i],
             send_sem=halo_send.at[i],
             recv_sem=halo_recv.at[i],
-            device_id={"seq": lax.rem(me + 1, parts)},
+            device_id=after,
         )
-        for i, stream in enumerate((q_in, k_in, v_in))
+        for i, source in enumerate((tail_kv, q_in.at[pl.ds(rows - GROUP, GROUP), :]))
     ]
-    for i in (1, 2, 0):
-        halo_copies[i].start()
+    tails[0].start()
 
     def own_rows(peer, h):
         return pl.ds(pl.multiple_of(peer * own + h * GROUP, GROUP), GROUP)
 
+    x, y, core = me // 8, lax.rem(me // 2, 4), lax.rem(me, 2)
+    peers = [
+        lax.rem(x + dx, 4) * 8 + lax.rem(y + dy, 4) * 2 + lax.rem(core + dc, 2)
+        for dx, dy, dc in STEPS
+    ]
+
     def exchange(source, target, send_sem, recv_sem):
         pltpu.make_async_copy(source(me), target, recv_sem).start()
-
-        @pl.loop(1, parts)
-        def _(d):
-            peer = lax.rem(me + d, parts)
+        for peer in peers:
             pltpu.make_async_remote_copy(
                 src_ref=source(peer),
                 dst_ref=target,
@@ -243,12 +257,12 @@
             lambda peer: send_f.at[own_rows(peer, h)], got_f.at[h, me], f_send.at[h], f_recv.at[h]
         )
 
-    for i in (1, 2):
-        halo_copies[i].wait_recv()
+    tails[0].wait_recv()
+    first = me == 0
+    head = jnp.where(first, 0.0, halo[0].astype(F32))
+    ext[1, pl.ds(0, 8), :] = head[:8]
+    ext[2, pl.ds(0, 8), :] = head[8:]
     loads[5].wait()
-    first = me == 0
-    for i in (1, 2):
-        ext[i, pl.ds(0, 8), :] = jnp.where(first, 0.0, halo[i].astype(F32)[8:, :])
 
     def short(i, b):
         weights = short_weight[i, :, lanes(b)].astype(F32)
@@ -268,8 +282,9 @@
             lambda peer: send_m.at[own_rows(peer, h)], got_m.at[h, me], m_send.at[h], m_recv.at[h]
         )
 
-    halo_copies[0].wait_recv()
-    ext[0, pl.ds(0, 8), :] = jnp.where(first, 0.0, halo[0].astype(F32)[8:, :])
+    tails[1].start()
+    tails[1].wait_recv()
+    ext[0, pl.ds(0, 8), :] = jnp.where(first, 0.0, halo[1].astype(F32))[8:]
     loads[4].wait()
     loads[6].wait()
 
@@ -311,6 +326,7 @@
 
     @pl.loop(0, halves)
     def _(h):
+        pass
         pltpu.make_async_copy(got_m.at[h], got_m.at[h], m_recv.at[h]).wait()
         first_stage(got_m, h)
         for c in range(ROWS // CHUNK):
@@ -338,19 +354,14 @@
     for b in range(blocks):
         at = pl.ds(b * LANES, LANES)
         conv = got_y[at, :].astype(F32).T
-        rounded = (base[:, at] + short_q[:, at] * conv).astype(BF16)
-        out_bf[:, at] = rounded
-        value = rounded.astype(F32)
-        stream_f[:, at] = value
+        total = base[:, at] + short_q[:, at] * conv
+        value = total.astype(BF16).astype(F32)
+        total_f[:, at] = value
         partial = partial + value * value
-    write_stream = pltpu.make_async_copy(out_bf, stream_out, out_sem.at[0])
-    write_stream.start()
-
     own_sum[...] = jnp.broadcast_to(jnp.sum(partial.T, axis=0, keepdims=True), own_sum.shape)
     pltpu.make_async_copy(own_sum, sums.at[plane], p_recv).start()
 
-    @pl.loop(1, rounds)
-    def _(d):
+    for d in sorted(range(1, rounds), key=lambda d: -min(d, rounds - d)):
         pltpu.make_async_remote_copy(
             src_ref=own_sum,
             dst_ref=sums.at[plane],
@@ -362,25 +373,19 @@
     pltpu.make_async_copy(sums, sums, p_recv).wait()
     power = jnp.sum(sums[...], axis=0)[0:1] / (width * rounds)
     loads[7].wait()
-    scale = jnp.broadcast_to(lax.rsqrt(power + 1e-05), (LANES, rows)).T
-    for b in range(blocks):
-        at = pl.ds(b * LANES, LANES)
-        norm_bf[:, at] = (stream_f[:, at] * scale * norm_gain[:, at]).astype(BF16)
-    write_normed = pltpu.make_async_copy(norm_bf, normed, out_sem.at[1])
-    write_normed.start()
-
-    for copy in halo_copies:
+    scale_v[...] = lax.rsqrt(power + 1e-05)
+
+    for copy in tails:
         copy.wait_send()
     others = pl.ds(0, parts - 1)
     for h in range(halves):
+        pass
         pltpu.make_async_copy(got_f.at[h, others], got_f.at[h, others], f_send.at[h]).wait()
         pltpu.make_async_copy(got_m.at[h, others], got_m.at[h, others], m_send.at[h]).wait()
         pltpu.make_async_copy(got_m.at[h, others], got_m.at[h, others], y_send.at[h]).wait()
     if rounds > 1:
         most = sums.at[pl.ds(0, rounds - 1)]
         pltpu.make_async_copy(most, most, p_send).wait()
-    write_stream.wait()
-    write_normed.wait()
 
 
 def shards(queries, keys, values, filters, short_weight, skip_gain, residual, norm_gain):
@@ -393,12 +398,14 @@
     matrices, twist = tables()
     block = (rows, width)
     whole = pl.BlockSpec(memory_space=pltpu.HBM)
+    near = pl.BlockSpec(memory_space=pltpu.VMEM)
     dma = pltpu.SemaphoreType.DMA
-    return pl.pallas_call(
+    fixed = lambda a: pltpu.with_memory_space_constraint(a, pltpu.HBM)
+    total, scale, gain = pl.pallas_call(
         kernel,
-        out_shape=(jax.ShapeDtypeStruct(block, BF16), jax.ShapeDtypeStruct(block, BF16)),
+        out_shape=(jax.ShapeDtypeStruct(block, F32), jax.ShapeDtypeStruct((1, rows), F32), jax.ShapeDtypeStruct((1, width), F32)),
         in_specs=[whole] * 10,
-        out_specs=(whole, whole),
+        out_specs=(near, near, near),
         scratch_shapes=[
             pltpu.VMEM(block, BF16),
             pltpu.VMEM(block, BF16),
@@ -406,18 +413,15 @@
             pltpu.VMEM(block, BF16),
             pltpu.VMEM(block, BF16),
             pltpu.VMEM((3, taps, width), BF16),
-            pltpu.VMEM((1, width), F32),
             pltpu.VMEM((1, width), F32),
             pltpu.VMEM(matrices.shape, BF16),
             pltpu.VMEM(twist.shape, F32),
-            pltpu.VMEM((3, GROUP, width), BF16),
+            pltpu.VMEM((GROUP, width), BF16),
+            pltpu.VMEM((2, GROUP, width), BF16),
             pltpu.VMEM((3, rows + 8, width), F32),
             pltpu.VMEM(block, BF16),
             pltpu.VMEM(block, F32),
             pltpu.VMEM(block, F32),
-            pltpu.VMEM(block, F32),
-            pltpu.VMEM(block, BF16),
-            pltpu.VMEM(block, BF16),
             pltpu.VMEM((width, rows), BF16),
             pltpu.VMEM((width, rows), BF16),
             pltpu.VMEM((halves, parts, GROUP, LANES), BF16),
@@ -431,8 +435,8 @@
             pltpu.VMEM((rounds, 8, LANES), F32),
             pltpu.VMEM((8, LANES), F32),
             dma((10,)),
-            dma((3,)),
-            dma((3,)),
+            dma((2,)),
+            dma((2,)),
             dma((halves,)),
             dma((halves,)),
             dma((halves,)),
@@ -441,16 +445,23 @@
             dma,
             dma,
             dma,
-            dma((2,)),
         ],
         compiler_params=pltpu.CompilerParams(
-            collective_id=0, has_side_effects=True, vmem_limit_bytes=60 * 1024 * 1024
+            collective_id=0, has_side_effects=True, vmem_limit_bytes=32 * 1024 * 1024
         ),
         cost_estimate=pl.CostEstimate(flops=2 * 10**9, bytes_accessed=2 * 10**6, transcendentals=0),
     )(
-        queries, keys, values, filters, short_weight, skip_gain[None, :], residual, norm_gain[None, :],
-        jnp.asarray(matrices), jnp.asarray(twist),
+        *[
+            fixed(a)
+            for a in (
+                queries, keys, values, filters, short_weight, skip_gain[None, :], residual, norm_gain[None, :],
+                jnp.asarray(matrices), jnp.asarray(twist),
+            )
+        ]
     )
+    stream_out = total.astype(BF16)
+    normed = (stream_out.astype(F32) * scale[0][:, None] * gain[0]).astype(BF16)
+    return stream_out, normed
 
 
 def solution(mesh):

time: 38.2 us -> 33.9 us (0.89)
  Pallas kernels: 35 us -> 32.4 us
  local copies, waits for them, and re-layouts: 2.42 us -> 0 us
  other arithmetic: 0 us -> 0.83 us
    pallas_call x1, Pallas kernels: 35 us -> 32.4 us  [shards(): pl.pallas_call(kernel, out_shape=(jax.ShapeDtypeStruct(block, F32), jax.S...]
    unnamed x4 -> x0, local copies, waits for them, and re-layouts: 2.42 us -> none
    convert_element_type x0 -> x1, other arithmetic: none -> 0.83 us  [shards(): normed = (stream_out.astype(F32) * scale[0][:, None] * gain[0]).astype(BF16)]
where the time goes in v1:
time: 33.9 us; the launch traced here: 33.8 us
  Pallas kernels  32.4 us (96%)
  other arithmetic  0.83 us (2%)
  between operations  0.64 us (2%)
    pallas_call x1, Pallas kernels, shards(): pl.pallas_call(kernel, out_shape=(jax.ShapeDtypeStruct(block, F32), jax.S...  32.4 us
    convert_element_type x1, other arithmetic, shards(): normed = (stream_out.astype(F32) * scale[0][:, None] * gain[0]).astype(BF16)  0.83 us

profile of v1, /device:TPU:1, one launch (start us, length us, event | category | flops | bytes accessed | tf_op | source)
XLA Modules:
  0.0 33.8 jit_solution(4918505928432754255)
XLA Ops:
  0.6 32.4 %shard_map.113 = (f32[128,1024]{1,0:T(8,128)S(1)}, f32[1,128]{1,0:T(1,128)S(1)}, f32[1,1024]{1,0:T(1,128)S(1)}) custom-call(bf16[128,1024]{1,0:T(8,128)(2,1)} %queries.1, bf16[128,1024]{1,0:T(8,128)(2,1)} %keys.1, bf16[128,1024]{1,0:T(8,128)(2,1)} %values.1, bf16[128,1024]{1,0:T(8,128)(2,1)} %filters.1, bf16[3,7,1024]{2,1,0:T(8,128)(2,1)} %short_taps.1, ...), custom_call_target="tpu_custom_call" | custom-call | flops 2000000000 | bytes 2000000 | tf_op jit(solution)/shard_map/pallas_call | solution.py:404
  33.0 0.8 %multiply_convert_fusion = (bf16[128,1024]{1,0:T(8,128)(2,1)}, bf16[128,1024]{1,0:T(8,128)(2,1)}) fusion(f32[1024]{0:T(1024)S(1)} %bitcast.4, f32[128]{0:T(128)S(1)} %bitcast.5, f32[128,1024]{1,0:T(8,128)S(1)} %get-tuple-element.5), kind=kLoop, calls=%fused_computation | loop fusion | flops 655360 | bytes 1053184 | tf_op jit(solution)/shard_map/convert_element_type | solution.py:463

commit v2 on v1

--- a/solution.py
+++ b/solution.py
@@ -177,9 +177,13 @@
 
     barrier = pltpu.get_barrier_semaphore()
 
-    @pl.loop(1, parts)
-    def _(d):
-        pl.semaphore_signal(barrier, inc=1, device_id={"seq": lax.rem(me + d, parts)})
+    x, y, core = me // 8, lax.rem(me // 2, 4), lax.rem(me, 2)
+    peers = [
+        lax.rem(x + dx, 4) * 8 + lax.rem(y + dy, 4) * 2 + lax.rem(core + dc, 2)
+        for dx, dy, dc in STEPS
+    ]
+    for peer in peers:
+        pl.semaphore_signal(barrier, inc=1, device_id={"seq": peer})
 
     @pl.loop(1, rounds)
     def _(d):
@@ -205,7 +209,7 @@
 
     @pl.loop(0, blocks)
     def _(b):
-        send_f[lanes(b), :] = f_in[:, lanes(b)].astype(F32).T.astype(BF16)
+        send_f[lanes(b), :] = f_in[:, lanes(b)].T
 
     for i in (1, 2, 3):
         loads[i].wait()
@@ -235,12 +239,6 @@
     def own_rows(peer, h):
         return pl.ds(pl.multiple_of(peer * own + h * GROUP, GROUP), GROUP)
 
-    x, y, core = me // 8, lax.rem(me // 2, 4), lax.rem(me, 2)
-    peers = [
-        lax.rem(x + dx, 4) * 8 + lax.rem(y + dy, 4) * 2 + lax.rem(core + dc, 2)
-        for dx, dy, dc in STEPS
-    ]
-
     def exchange(source, target, send_sem, recv_sem):
         pltpu.make_async_copy(source(me), target, recv_sem).start()
         for peer in peers:
@@ -257,25 +255,34 @@
             lambda peer: send_f.at[own_rows(peer, h)], got_f.at[h, me], f_send.at[h], f_recv.at[h]
         )
 
+    def short(i, b, count):
+        weights = short_weight[i, :, lanes(b)].astype(F32)
+        total = weights[0:1] * ext[i, pl.ds(8, count), lanes(b)]
+        for j in range(1, weights.shape[0]):
+            total = total + weights[j : j + 1] * ext[i, pl.ds(8 - j, count), lanes(b)]
+        return total
+
+    loads[5].wait()
+    for i in range(3):
+        ext[i, pl.ds(0, 8), :] = jnp.zeros((8, width), F32)
+
+    @pl.loop(0, blocks)
+    def _(b):
+        product = short(1, b, rows) * short(2, b, rows)
+        mixed[:, lanes(b)] = product.astype(BF16)
+        send_m[lanes(b), :] = product.astype(BF16).T
+
     tails[0].wait_recv()
     first = me == 0
     head = jnp.where(first, 0.0, halo[0].astype(F32))
     ext[1, pl.ds(0, 8), :] = head[:8]
     ext[2, pl.ds(0, 8), :] = head[8:]
-    loads[5].wait()
-
-    def short(i, b):
-        weights = short_weight[i, :, lanes(b)].astype(F32)
-        total = weights[0:1] * ext[i, pl.ds(8, rows), lanes(b)]
-        for j in range(1, weights.shape[0]):
-            total = total + weights[j : j + 1] * ext[i, pl.ds(8 - j, rows), lanes(b)]
-        return total
 
     @pl.loop(0, blocks)
     def _(b):
-        product = (short(1, b) * short(2, b)).astype(BF16)
-        mixed[:, lanes(b)] = product
-        send_m[lanes(b), :] = product.astype(F32).T.astype(BF16)
+        product = short(1, b, GROUP) * short(2, b, GROUP)
+        mixed[pl.ds(0, GROUP), lanes(b)] = product.astype(BF16)
+        send_m[lanes(b), pl.ds(0, GROUP)] = product.astype(BF16).T
 
     for h in range(halves):
         exchange(
@@ -283,18 +290,6 @@
         )
 
     tails[1].start()
-    tails[1].wait_recv()
-    ext[0, pl.ds(0, 8), :] = jnp.where(first, 0.0, halo[1].astype(F32))[8:]
-    loads[4].wait()
-    loads[6].wait()
-
-    @pl.loop(0, blocks)
-    def _(b):
-        gate = short(0, b)
-        short_q[:, lanes(b)] = gate
-        direct = skip_gain[:, lanes(b)] * mixed[:, lanes(b)].astype(F32)
-        base[:, lanes(b)] = r_in[:, lanes(b)].astype(F32) + gate * direct
-
     loads[8].wait()
     loads[9].wait()
 
@@ -348,12 +343,24 @@
             send_y[h, s] = y.astype(BF16)
         exchange(lambda peer: send_y.at[h, peer], got_y.at[own_rows(me, h)], y_send.at[h], y_recv)
 
+    tails[1].wait_recv()
+    ext[0, pl.ds(0, 8), :] = jnp.where(first, 0.0, halo[1].astype(F32))[8:]
+    loads[4].wait()
+    loads[6].wait()
+
+    @pl.loop(0, blocks)
+    def _(b):
+        gate = short(0, b, rows)
+        short_q[:, lanes(b)] = gate
+        direct = skip_gain[:, lanes(b)] * mixed[:, lanes(b)].astype(F32)
+        base[:, lanes(b)] = r_in[:, lanes(b)].astype(F32) + gate * direct
+
     pltpu.make_async_copy(got_y, got_y, y_recv).wait()
 
     partial = jnp.zeros((rows, LANES), F32)
     for b in range(blocks):
         at = pl.ds(b * LANES, LANES)
-        conv = got_y[at, :].astype(F32).T
+        conv = got_y[at, :].T.astype(F32)
         total = base[:, at] + short_q[:, at] * conv
         value = total.astype(BF16).astype(F32)
         total_f[:, at] = value

time: 33.9 us -> 32.8 us (0.968)
  Pallas kernels: 32.4 us -> 31.3 us
    pallas_call x1, Pallas kernels: 32.4 us -> 31.3 us  [shards(): pl.pallas_call(kernel, out_shape=(jax.ShapeDtypeStruct(block, F32), jax.S...]
where the time goes in v2:
time: 32.8 us; the launch traced here: 32.7 us
  Pallas kernels  31.3 us (95%)
  other arithmetic  0.83 us (3%)
  between operations  0.64 us (2%)
    pallas_call x1, Pallas kernels, shards(): pl.pallas_call(kernel, out_shape=(jax.ShapeDtypeStruct(block, F32), jax.S...  31.3 us
    convert_element_type x1, other arithmetic, shards(): normed = (stream_out.astype(F32) * scale[0][:, None] * gain[0]).astype(BF16)  0.83 us

profile of v2, /device:TPU:1, one launch (start us, length us, event | category | flops | bytes accessed | tf_op | source)
XLA Modules:
  0.0 32.7 jit_solution(4678205998668779431)
XLA Ops:
  0.6 31.3 %shard_map.113 = (f32[128,1024]{1,0:T(8,128)S(1)}, f32[1,128]{1,0:T(1,128)S(1)}, f32[1,1024]{1,0:T(1,128)S(1)}) custom-call(bf16[128,1024]{1,0:T(8,128)(2,1)} %queries.1, bf16[128,1024]{1,0:T(8,128)(2,1)} %keys.1, bf16[128,1024]{1,0:T(8,128)(2,1)} %values.1, bf16[128,1024]{1,0:T(8,128)(2,1)} %filters.1, bf16[3,7,1024]{2,1,0:T(8,128)(2,1)} %short_taps.1, ...), custom_call_target="tpu_custom_call" | custom-call | flops 2000000000 | bytes 2000000 | tf_op jit(solution)/shard_map/pallas_call | solution.py:411
  31.9 0.8 %multiply_convert_fusion = (bf16[128,1024]{1,0:T(8,128)(2,1)}, bf16[128,1024]{1,0:T(8,128)(2,1)}) fusion(f32[1024]{0:T(1024)S(1)} %bitcast.4, f32[128]{0:T(128)S(1)} %bitcast.5, f32[128,1024]{1,0:T(8,128)S(1)} %get-tuple-element.5), kind=kLoop, calls=%fused_computation | loop fusion | flops 655360 | bytes 1053184 | tf_op jit(solution)/shard_map/convert_element_type | solution.py:470

commit v3 on v2

--- a/solution.py
+++ b/solution.py
@@ -32,6 +32,9 @@
     ((dx, dy, dc) for dx in range(4) for dy in range(4) for dc in range(2) if dx + dy + dc > 0),
     key=lambda step: -(min(step[0], 4 - step[0]) + min(step[1], 4 - step[1])),
 )
+
+
+ABS = sorted(range(32), key=lambda p: (p // 8 + p // 2 % 4, -(p % 2)))
 
 
 def tables():
@@ -45,7 +48,7 @@
         high = matrix.astype(np.float32).astype(jnp.bfloat16)
         low = (matrix - high.astype(np.float64)).astype(np.float32).astype(jnp.bfloat16)
         parts += [high, low]
-    matrices = np.stack(parts)
+    matrices = np.stack(parts[:3])
     turn = 2.0 * np.pi * np.outer(KEPT, lane) / (64 * LANES)
     weight = np.where(np.isin(KEPT, [0, 32]), 1.0, 2.0)[:, None] / (64 * LANES)
     twist = np.stack([np.cos(turn), -np.sin(turn), weight * np.cos(turn), weight * np.sin(turn)])
@@ -156,9 +159,12 @@
     return high, (a - high.astype(F32)).astype(BF16)
 
 
+def matmul(a, matrix):
+    return jnp.dot(a, matrix, preferred_element_type=F32)
+
+
 def product3(high, low, matrix_high, matrix_low):
-    dot = functools.partial(jnp.dot, preferred_element_type=F32)
-    return dot(high, matrix_high) + (dot(low, matrix_high) + dot(high, matrix_low))
+    return matmul(high, matrix_high) + (matmul(low, matrix_high) + matmul(high, matrix_low))
 
 
 def kernel(
@@ -213,9 +219,6 @@
 
     for i in (1, 2, 3):
         loads[i].wait()
-    for i, stream in enumerate((q_in, k_in, v_in)):
-        ext[i, pl.ds(8, rows), :] = stream[...].astype(F32)
-
     last = pl.ds(rows - GROUP, GROUP)
     tail_kv[...] = jnp.concatenate(
         [k_in[last, :].astype(F32)[8:], v_in[last, :].astype(F32)[8:]], axis=0
@@ -237,7 +240,20 @@
     tails[0].start()
 
     def own_rows(peer, h):
-        return pl.ds(pl.multiple_of(peer * own + h * GROUP, GROUP), GROUP)
+        return pl.ds(pl.multiple_of(h * (width // halves) + peer * GROUP, GROUP), GROUP)
+
+    def exchange_abs(source, target, send_sem, recv_sem):
+        pltpu.make_async_copy(source(me), target, recv_sem).start()
+        for peer in ABS:
+            @pl.when(me != peer)
+            def _():
+                pltpu.make_async_remote_copy(
+                    src_ref=source(peer),
+                    dst_ref=target,
+                    send_sem=send_sem,
+                    recv_sem=recv_sem,
+                    device_id={"seq": peer},
+                ).start()
 
     def exchange(source, target, send_sem, recv_sem):
         pltpu.make_async_copy(source(me), target, recv_sem).start()
@@ -255,6 +271,9 @@
             lambda peer: send_f.at[own_rows(peer, h)], got_f.at[h, me], f_send.at[h], f_recv.at[h]
         )
 
+    for i, stream in enumerate((q_in, k_in, v_in)):
+        ext[i, pl.ds(8, rows), :] = stream[...].astype(F32)
+
     def short(i, b, count):
         weights = short_weight[i, :, lanes(b)].astype(F32)
         total = weights[0:1] * ext[i, pl.ds(8, count), lanes(b)]
@@ -278,13 +297,14 @@
     ext[1, pl.ds(0, 8), :] = head[:8]
     ext[2, pl.ds(0, 8), :] = head[8:]
 
-    @pl.loop(0, blocks)
-    def _(b):
-        product = short(1, b, GROUP) * short(2, b, GROUP)
-        mixed[pl.ds(0, GROUP), lanes(b)] = product.astype(BF16)
-        send_m[lanes(b), pl.ds(0, GROUP)] = product.astype(BF16).T
-
     for h in range(halves):
+
+        @pl.loop(h * blocks // halves, (h + 1) * blocks // halves)
+        def _(b):
+            product = short(1, b, GROUP) * short(2, b, GROUP)
+            mixed[pl.ds(0, GROUP), lanes(b)] = product.astype(BF16)
+            send_m[lanes(b), pl.ds(0, GROUP)] = product.astype(BF16).T
+
         exchange(
             lambda peer: send_m.at[own_rows(peer, h)], got_m.at[h, me], m_send.at[h], m_recv.at[h]
         )
@@ -299,22 +319,23 @@
             return value[0] * cos, value[0] * sin
         return value[0] * cos - value[1] * sin, value[1] * cos + value[0] * sin
 
-    def first_stage(got, h):
+    def first_stage(got, h, low):
         spectrum = forward64([got[h, s].astype(F32) for s in range(PARTS)])
         for k1 in KEPT:
             i = PLACE[k1]
             for half, part in enumerate(twisted(spectrum[k1], i, 0)):
-                high, low = split(part)
                 place = (pl.ds(i * GROUP, GROUP), pl.ds(half * LANES, LANES))
-                a_high[place] = high
-                a_low[place] = low
+                if low:
+                    a_high[place], a_low[place] = split(part)
+                else:
+                    a_high[place] = part.astype(BF16)
 
     for h in range(halves):
         pltpu.make_async_copy(got_f.at[h], got_f.at[h], f_recv.at[h]).wait()
 
     @pl.loop(0, halves)
     def _(h):
-        first_stage(got_f, h)
+        first_stage(got_f, h, True)
         for c in range(ROWS // CHUNK):
             chunk = pl.ds(c * CHUNK, CHUNK)
             spec_f[h, chunk, :] = product3(a_high[chunk, :], a_low[chunk, :], mat[0], mat[1])
@@ -323,16 +344,15 @@
     def _(h):
         pass
         pltpu.make_async_copy(got_m.at[h], got_m.at[h], m_recv.at[h]).wait()
-        first_stage(got_m, h)
+        first_stage(got_m, h, False)
         for c in range(ROWS // CHUNK):
             chunk = pl.ds(c * CHUNK, CHUNK)
-            signal = product3(a_high[chunk, :], a_low[chunk, :], mat[0], mat[1])
+            signal = matmul(a_high[chunk, :], mat[0])
             taps = spec_f[h, chunk, :]
             sr, si = signal[:, :LANES], signal[:, LANES:]
             fr, fi = taps[:, :LANES], taps[:, LANES:]
             both = jnp.concatenate([sr * fr - si * fi, sr * fi + si * fr], axis=1)
-            high, low = split(both)
-            back[chunk, :] = product3(high, low, mat[2], mat[3])
+            back[chunk, :] = matmul(both.astype(BF16), mat[2])
 
         def value(k1):
             i = PLACE[k1]
@@ -341,7 +361,7 @@
 
         for s, y in enumerate(backward64(value)):
             send_y[h, s] = y.astype(BF16)
-        exchange(lambda peer: send_y.at[h, peer], got_y.at[own_rows(me, h)], y_send.at[h], y_recv)
+        exchange_abs(lambda peer: send_y.at[h, peer], got_y.at[own_rows(me, h)], y_send.at[h], y_recv.at[h])
 
     tails[1].wait_recv()
     ext[0, pl.ds(0, 8), :] = jnp.where(first, 0.0, halo[1].astype(F32))[8:]
@@ -355,16 +375,17 @@
         direct = skip_gain[:, lanes(b)] * mixed[:, lanes(b)].astype(F32)
         base[:, lanes(b)] = r_in[:, lanes(b)].astype(F32) + gate * direct
 
-    pltpu.make_async_copy(got_y, got_y, y_recv).wait()
-
     partial = jnp.zeros((rows, LANES), F32)
-    for b in range(blocks):
-        at = pl.ds(b * LANES, LANES)
-        conv = got_y[at, :].T.astype(F32)
-        total = base[:, at] + short_q[:, at] * conv
-        value = total.astype(BF16).astype(F32)
-        total_f[:, at] = value
-        partial = partial + value * value
+    for h in range(halves):
+        arrived = got_y.at[pl.ds(h * (width // halves), width // halves)]
+        pltpu.make_async_copy(arrived, arrived, y_recv.at[h]).wait()
+        for b in range(h * blocks // halves, (h + 1) * blocks // halves):
+            at = pl.ds(b * LANES, LANES)
+            conv = got_y[at, :].T.astype(F32)
+            value = (base[:, at] + short_q[:, at] * conv).astype(BF16).astype(F32)
+            total_f[:, at] = value
+            partial = partial + value * value
+
     own_sum[...] = jnp.broadcast_to(jnp.sum(partial.T, axis=0, keepdims=True), own_sum.shape)
     pltpu.make_async_copy(own_sum, sums.at[plane], p_recv).start()
 
@@ -449,7 +470,7 @@
             dma((halves,)),
             dma((halves,)),
             dma((halves,)),
-            dma,
+            dma((halves,)),
             dma,
             dma,
         ],

time: 32.8 us -> 31.8 us (0.970)
  Pallas kernels: 31.3 us -> 30.3 us
    pallas_call x1, Pallas kernels: 31.3 us -> 30.3 us  [shards(): pl.pallas_call(kernel, out_shape=(jax.ShapeDtypeStruct(block, F32), jax.S...]
where the time goes in v3:
time: 31.8 us; the launch traced here: 31.7 us
  Pallas kernels  30.3 us (95%)
  other arithmetic  0.83 us (3%)
  between operations  0.64 us (2%)
    pallas_call x1, Pallas kernels, shards(): pl.pallas_call(kernel, out_shape=(jax.ShapeDtypeStruct(block, F32), jax.S...  30.3 us
    convert_element_type x1, other arithmetic, shards(): normed = (stream_out.astype(F32) * scale[0][:, None] * gain[0]).astype(BF16)  0.83 us

profile of v3, /device:TPU:1, one launch (start us, length us, event | category | flops | bytes accessed | tf_op | source)
XLA Modules:
  0.0 31.7 jit_solution(4913075033272737486)
XLA Ops:
  0.6 30.3 %shard_map.113 = (f32[128,1024]{1,0:T(8,128)S(1)}, f32[1,128]{1,0:T(1,128)S(1)}, f32[1,1024]{1,0:T(1,128)S(1)}) custom-call(bf16[128,1024]{1,0:T(8,128)(2,1)} %queries.1, bf16[128,1024]{1,0:T(8,128)(2,1)} %keys.1, bf16[128,1024]{1,0:T(8,128)(2,1)} %values.1, bf16[128,1024]{1,0:T(8,128)(2,1)} %filters.1, bf16[3,7,1024]{2,1,0:T(8,128)(2,1)} %short_taps.1, ...), custom_call_target="tpu_custom_call" | custom-call | flops 2000000000 | bytes 2000000 | tf_op jit(solution)/shard_map/pallas_call | solution.py:432
  30.9 0.8 %multiply_convert_fusion = (bf16[128,1024]{1,0:T(8,128)(2,1)}, bf16[128,1024]{1,0:T(8,128)(2,1)}) fusion(f32[1024]{0:T(1024)S(1)} %bitcast.4, f32[128]{0:T(128)S(1)} %bitcast.5, f32[128,1024]{1,0:T(8,128)S(1)} %get-tuple-element.5), kind=kLoop, calls=%fused_computation | loop fusion | flops 655360 | bytes 1053184 | tf_op jit(solution)/shard_map/convert_element_type | solution.py:491

commit v4 on v3

--- a/solution.py
+++ b/solution.py
@@ -48,7 +48,7 @@
         high = matrix.astype(np.float32).astype(jnp.bfloat16)
         low = (matrix - high.astype(np.float64)).astype(np.float32).astype(jnp.bfloat16)
         parts += [high, low]
-    matrices = np.stack(parts[:3])
+    matrices = np.stack(parts)
     turn = 2.0 * np.pi * np.outer(KEPT, lane) / (64 * LANES)
     weight = np.where(np.isin(KEPT, [0, 32]), 1.0, 2.0)[:, None] / (64 * LANES)
     twist = np.stack([np.cos(turn), -np.sin(turn), weight * np.cos(turn), weight * np.sin(turn)])
@@ -238,6 +238,7 @@
         for i, source in enumerate((tail_kv, q_in.at[pl.ds(rows - GROUP, GROUP), :]))
     ]
     tails[0].start()
+    tails[1].start()
 
     def own_rows(peer, h):
         return pl.ds(pl.multiple_of(h * (width // halves) + peer * GROUP, GROUP), GROUP)
@@ -309,7 +310,6 @@
             lambda peer: send_m.at[own_rows(peer, h)], got_m.at[h, me], m_send.at[h], m_recv.at[h]
         )
 
-    tails[1].start()
     loads[8].wait()
     loads[9].wait()
 
@@ -319,23 +319,18 @@
             return value[0] * cos, value[0] * sin
         return value[0] * cos - value[1] * sin, value[1] * cos + value[0] * sin
 
-    def first_stage(got, h, low):
+    def first_stage(got, h):
         spectrum = forward64([got[h, s].astype(F32) for s in range(PARTS)])
         for k1 in KEPT:
             i = PLACE[k1]
             for half, part in enumerate(twisted(spectrum[k1], i, 0)):
                 place = (pl.ds(i * GROUP, GROUP), pl.ds(half * LANES, LANES))
-                if low:
-                    a_high[place], a_low[place] = split(part)
-                else:
-                    a_high[place] = part.astype(BF16)
-
-    for h in range(halves):
-        pltpu.make_async_copy(got_f.at[h], got_f.at[h], f_recv.at[h]).wait()
+                a_high[place], a_low[place] = split(part)
 
     @pl.loop(0, halves)
     def _(h):
-        first_stage(got_f, h, True)
+        pltpu.make_async_copy(got_f.at[h], got_f.at[h], f_recv.at[h]).wait()
+        first_stage(got_f, h)
         for c in range(ROWS // CHUNK):
             chunk = pl.ds(c * CHUNK, CHUNK)
             spec_f[h, chunk, :] = product3(a_high[chunk, :], a_low[chunk, :], mat[0], mat[1])
@@ -344,15 +339,15 @@
     def _(h):
         pass
         pltpu.make_async_copy(got_m.at[h], got_m.at[h], m_recv.at[h]).wait()
-        first_stage(got_m, h, False)
+        first_stage(got_m, h)
         for c in range(ROWS // CHUNK):
             chunk = pl.ds(c * CHUNK, CHUNK)
-            signal = matmul(a_high[chunk, :], mat[0])
+            signal = product3(a_high[chunk, :], a_low[chunk, :], mat[0], mat[1])
             taps = spec_f[h, chunk, :]
             sr, si = signal[:, :LANES], signal[:, LANES:]
             fr, fi = taps[:, :LANES], taps[:, LANES:]
             both = jnp.concatenate([sr * fr - si * fi, sr * fi + si * fr], axis=1)
-            back[chunk, :] = matmul(both.astype(BF16), mat[2])
+            back[chunk, :] = product3(*split(both), mat[2], mat[3])
 
         def value(k1):
             i = PLACE[k1]
@@ -386,7 +381,7 @@
             total_f[:, at] = value
             partial = partial + value * value
 
-    own_sum[...] = jnp.broadcast_to(jnp.sum(partial.T, axis=0, keepdims=True), own_sum.shape)
+    own_sum[...] = jnp.sum(partial.T, axis=0, keepdims=True)
     pltpu.make_async_copy(own_sum, sums.at[plane], p_recv).start()
 
     for d in sorted(range(1, rounds), key=lambda d: -min(d, rounds - d)):
@@ -397,11 +392,6 @@
             recv_sem=p_recv,
             device_id={"ch": lax.rem(plane + d, rounds)},
         ).start()
-
-    pltpu.make_async_copy(sums, sums, p_recv).wait()
-    power = jnp.sum(sums[...], axis=0)[0:1] / (width * rounds)
-    loads[7].wait()
-    scale_v[...] = lax.rsqrt(power + 1e-05)
 
     for copy in tails:
         copy.wait_send()
@@ -414,6 +404,11 @@
     if rounds > 1:
         most = sums.at[pl.ds(0, rounds - 1)]
         pltpu.make_async_copy(most, most, p_send).wait()
+    loads[7].wait()
+
+    pltpu.make_async_copy(sums, sums, p_recv).wait()
+    power = jnp.sum(sums[...], axis=0) / (width * rounds)
+    scale_v[...] = lax.rsqrt(power + 1e-05)
 
 
 def shards(queries, keys, values, filters, short_weight, skip_gain, residual, norm_gain):
@@ -460,8 +455,8 @@
             pltpu.VMEM((ROWS, 2 * LANES), BF16),
             pltpu.VMEM((halves, ROWS, 2 * LANES), F32),
             pltpu.VMEM((ROWS, 2 * LANES), F32),
-            pltpu.VMEM((rounds, 8, LANES), F32),
-            pltpu.VMEM((8, LANES), F32),
+            pltpu.VMEM((rounds, 1, LANES), F32),
+            pltpu.VMEM((1, LANES), F32),
             dma((10,)),
             dma((2,)),
             dma((2,)),

time: 31.8 us -> 32.2 us (1.013)
  Pallas kernels: 30.3 us -> 30.7 us
    pallas_call x1, Pallas kernels: 30.3 us -> 30.7 us  [shards(): pl.pallas_call(kernel, out_shape=(jax.ShapeDtypeStruct(block, F32), jax.S...]
where the time goes in v4:
time: 32.2 us; the launch traced here: 32.1 us
  Pallas kernels  30.7 us (95%)
  other arithmetic  0.83 us (3%)
  between operations  0.64 us (2%)
    pallas_call x1, Pallas kernels, shards(): pl.pallas_call(kernel, out_shape=(jax.ShapeDtypeStruct(block, F32), jax.S...  30.7 us
    convert_element_type x1, other arithmetic, shards(): normed = (stream_out.astype(F32) * scale[0][:, None] * gain[0]).astype(BF16)  0.83 us

profile of v4, /device:TPU:1, one launch (start us, length us, event | category | flops | bytes accessed | tf_op | source)
XLA Modules:
  0.0 32.1 jit_solution(5387074729712343891)
XLA Ops:
  0.6 30.7 %shard_map.113 = (f32[128,1024]{1,0:T(8,128)S(1)}, f32[1,128]{1,0:T(1,128)S(1)}, f32[1,1024]{1,0:T(1,128)S(1)}) custom-call(bf16[128,1024]{1,0:T(8,128)(2,1)} %queries.1, bf16[128,1024]{1,0:T(8,128)(2,1)} %keys.1, bf16[128,1024]{1,0:T(8,128)(2,1)} %values.1, bf16[128,1024]{1,0:T(8,128)(2,1)} %filters.1, bf16[3,7,1024]{2,1,0:T(8,128)(2,1)} %short_taps.1, ...), custom_call_target="tpu_custom_call" | custom-call | flops 2000000000 | bytes 2000000 | tf_op jit(solution)/shard_map/pallas_call | solution.py:427
  31.3 0.8 %multiply_convert_fusion = (bf16[128,1024]{1,0:T(8,128)(2,1)}, bf16[128,1024]{1,0:T(8,128)(2,1)}) fusion(f32[1024]{0:T(1024)S(1)} %bitcast.4, f32[128]{0:T(128)S(1)} %bitcast.5, f32[128,1024]{1,0:T(8,128)S(1)} %get-tuple-element.5), kind=kLoop, calls=%fused_computation | loop fusion | flops 655360 | bytes 1053184 | tf_op jit(solution)/shard_map/convert_element_type | solution.py:486

commit v5 on v4

--- a/solution.py
+++ b/solution.py
@@ -324,7 +324,7 @@
         for k1 in KEPT:
             i = PLACE[k1]
             for half, part in enumerate(twisted(spectrum[k1], i, 0)):
-                place = (pl.ds(i * GROUP, GROUP), pl.ds(half * LANES, LANES))
+                place = (h, pl.ds(i * GROUP, GROUP), pl.ds(half * LANES, LANES))
                 a_high[place], a_low[place] = split(part)
 
     @pl.loop(0, halves)
@@ -333,30 +333,41 @@
         first_stage(got_f, h)
         for c in range(ROWS // CHUNK):
             chunk = pl.ds(c * CHUNK, CHUNK)
-            spec_f[h, chunk, :] = product3(a_high[chunk, :], a_low[chunk, :], mat[0], mat[1])
-
-    @pl.loop(0, halves)
-    def _(h):
-        pass
-        pltpu.make_async_copy(got_m.at[h], got_m.at[h], m_recv.at[h]).wait()
-        first_stage(got_m, h)
+            spec_f[h, chunk, :] = product3(a_high[h, chunk, :], a_low[h, chunk, :], mat[0], mat[1])
+
+    def middle(h):
         for c in range(ROWS // CHUNK):
             chunk = pl.ds(c * CHUNK, CHUNK)
-            signal = product3(a_high[chunk, :], a_low[chunk, :], mat[0], mat[1])
+            signal = product3(a_high[h, chunk, :], a_low[h, chunk, :], mat[0], mat[1])
             taps = spec_f[h, chunk, :]
             sr, si = signal[:, :LANES], signal[:, LANES:]
             fr, fi = taps[:, :LANES], taps[:, LANES:]
             both = jnp.concatenate([sr * fr - si * fi, sr * fi + si * fr], axis=1)
-            back[chunk, :] = product3(*split(both), mat[2], mat[3])
-
+            back[h, chunk, :] = product3(*split(both), mat[2], mat[3])
+
+    def last_stage(h):
         def value(k1):
             i = PLACE[k1]
             part = pl.ds(i * GROUP, GROUP)
-            return twisted((back[part, pl.ds(0, LANES)], back[part, pl.ds(LANES, LANES)]), i, 2)
+            return twisted(
+                (back[h, part, pl.ds(0, LANES)], back[h, part, pl.ds(LANES, LANES)]), i, 2
+            )
 
         for s, y in enumerate(backward64(value)):
             send_y[h, s] = y.astype(BF16)
-        exchange_abs(lambda peer: send_y.at[h, peer], got_y.at[own_rows(me, h)], y_send.at[h], y_recv.at[h])
+
+    for step in range(halves + 2):
+        if step < halves:
+            pltpu.make_async_copy(got_m.at[step], got_m.at[step], m_recv.at[step]).wait()
+            first_stage(got_m, step)
+        if 1 <= step <= halves:
+            middle(step - 1)
+        if step >= 2:
+            h = step - 2
+            last_stage(h)
+            exchange_abs(
+                lambda peer: send_y.at[h, peer], got_y.at[own_rows(me, h)], y_send.at[h], y_recv.at[h]
+            )
 
     tails[1].wait_recv()
     ext[0, pl.ds(0, 8), :] = jnp.where(first, 0.0, halo[1].astype(F32))[8:]
@@ -451,10 +462,10 @@
             pltpu.VMEM((halves, parts, GROUP, LANES), BF16),
             pltpu.VMEM((halves, parts, GROUP, LANES), BF16),
             pltpu.VMEM((width, rows), BF16),
-            pltpu.VMEM((ROWS, 2 * LANES), BF16),
-            pltpu.VMEM((ROWS, 2 * LANES), BF16),
+            pltpu.VMEM((halves, ROWS, 2 * LANES), BF16),
+            pltpu.VMEM((halves, ROWS, 2 * LANES), BF16),
             pltpu.VMEM((halves, ROWS, 2 * LANES), F32),
-            pltpu.VMEM((ROWS, 2 * LANES), F32),
+            pltpu.VMEM((halves, ROWS, 2 * LANES), F32),
             pltpu.VMEM((rounds, 1, LANES), F32),
             pltpu.VMEM((1, LANES), F32),
             dma((10,)),

time: 32.2 us -> 33.4 us (1.037)
  Pallas kernels: 30.7 us -> 31.8 us
    pallas_call x1, Pallas kernels: 30.7 us -> 31.8 us  [shards(): pl.pallas_call(kernel, out_shape=(jax.ShapeDtypeStruct(block, F32), jax.S...]
where the time goes in v5:
time: 33.4 us; the launch traced here: 33.3 us
  Pallas kernels  31.8 us (95%)
  other arithmetic  0.83 us (2%)
  between operations  0.64 us (2%)
    pallas_call x1, Pallas kernels, shards(): pl.pallas_call(kernel, out_shape=(jax.ShapeDtypeStruct(block, F32), jax.S...  31.8 us
    convert_element_type x1, other arithmetic, shards(): normed = (stream_out.astype(F32) * scale[0][:, None] * gain[0]).astype(BF16)  0.83 us

profile of v5, /device:TPU:1, one launch (start us, length us, event | category | flops | bytes accessed | tf_op | source)
XLA Modules:
  0.0 33.3 jit_solution(249142416703118537)
XLA Ops:
  0.6 31.8 %shard_map.113 = (f32[128,1024]{1,0:T(8,128)S(1)}, f32[1,128]{1,0:T(1,128)S(1)}, f32[1,1024]{1,0:T(1,128)S(1)}) custom-call(bf16[128,1024]{1,0:T(8,128)(2,1)} %queries.1, bf16[128,1024]{1,0:T(8,128)(2,1)} %keys.1, bf16[128,1024]{1,0:T(8,128)(2,1)} %values.1, bf16[128,1024]{1,0:T(8,128)(2,1)} %filters.1, bf16[3,7,1024]{2,1,0:T(8,128)(2,1)} %short_taps.1, ...), custom_call_target="tpu_custom_call" | custom-call | flops 2000000000 | bytes 2000000 | tf_op jit(solution)/shard_map/pallas_call | solution.py:438
  32.5 0.8 %multiply_convert_fusion = (bf16[128,1024]{1,0:T(8,128)(2,1)}, bf16[128,1024]{1,0:T(8,128)(2,1)}) fusion(f32[1024]{0:T(1024)S(1)} %bitcast.4, f32[128]{0:T(128)S(1)} %bitcast.5, f32[128,1024]{1,0:T(8,128)S(1)} %get-tuple-element.5), kind=kLoop, calls=%fused_computation | loop fusion | flops 655360 | bytes 1053184 | tf_op jit(solution)/shard_map/convert_element_type | solution.py:497

commit v6 on v4

--- a/solution.py
+++ b/solution.py
@@ -335,9 +335,6 @@
             chunk = pl.ds(c * CHUNK, CHUNK)
             spec_f[h, chunk, :] = product3(a_high[chunk, :], a_low[chunk, :], mat[0], mat[1])
 
-    @pl.loop(0, halves)
-    def _(h):
-        pass
         pltpu.make_async_copy(got_m.at[h], got_m.at[h], m_recv.at[h]).wait()
         first_stage(got_m, h)
         for c in range(ROWS // CHUNK):

time: 32.2 us -> 32.4 us (level)
  no operation moved by 1% of the time
where the time goes in v6:
time: 32.4 us; the launch traced here: 32.3 us
  Pallas kernels  30.8 us (95%)
  other arithmetic  0.83 us (3%)
  between operations  0.64 us (2%)
    pallas_call x1, Pallas kernels, shards(): pl.pallas_call(kernel, out_shape=(jax.ShapeDtypeStruct(block, F32), jax.S...  30.8 us
    convert_element_type x1, other arithmetic, shards(): normed = (stream_out.astype(F32) * scale[0][:, None] * gain[0]).astype(BF16)  0.83 us

profile of v6, /device:TPU:1, one launch (start us, length us, event | category | flops | bytes accessed | tf_op | source)
XLA Modules:
  0.0 32.3 jit_solution(15193913693896552197)
XLA Ops:
  0.6 30.8 %shard_map.113 = (f32[128,1024]{1,0:T(8,128)S(1)}, f32[1,128]{1,0:T(1,128)S(1)}, f32[1,1024]{1,0:T(1,128)S(1)}) custom-call(bf16[128,1024]{1,0:T(8,128)(2,1)} %queries.1, bf16[128,1024]{1,0:T(8,128)(2,1)} %keys.1, bf16[128,1024]{1,0:T(8,128)(2,1)} %values.1, bf16[128,1024]{1,0:T(8,128)(2,1)} %filters.1, bf16[3,7,1024]{2,1,0:T(8,128)(2,1)} %short_taps.1, ...), custom_call_target="tpu_custom_call" | custom-call | flops 2000000000 | bytes 2000000 | tf_op jit(solution)/shard_map/pallas_call | solution.py:424
  31.5 0.8 %multiply_convert_fusion = (bf16[128,1024]{1,0:T(8,128)(2,1)}, bf16[128,1024]{1,0:T(8,128)(2,1)}) fusion(f32[1024]{0:T(1024)S(1)} %bitcast.4, f32[128]{0:T(128)S(1)} %bitcast.5, f32[128,1024]{1,0:T(8,128)S(1)} %get-tuple-element.5), kind=kLoop, calls=%fused_computation | loop fusion | flops 655360 | bytes 1053184 | tf_op jit(solution)/shard_map/convert_element_type | solution.py:483

commit v7 on v4

--- a/solution.py
+++ b/solution.py
@@ -199,7 +199,7 @@
         pltpu.make_async_copy(source, target, in_sem.at[i])
         for i, (source, target) in enumerate(
             [
-                (filters, f_in), (keys, k_in), (values, v_in), (queries, q_in), (residual, r_in),
+                (keys, k_in), (values, v_in), (queries, q_in), (filters, f_in), (residual, r_in),
                 (short_taps, short_weight), (skip, skip_gain), (gain, gain_v),
                 (matrices, mat), (twist, tw),
             ]
@@ -211,13 +211,7 @@
     def lanes(b):
         return pl.ds(pl.multiple_of(b * LANES, LANES), LANES)
 
-    loads[0].wait()
-
-    @pl.loop(0, blocks)
-    def _(b):
-        send_f[lanes(b), :] = f_in[:, lanes(b)].T
-
-    for i in (1, 2, 3):
+    for i in (0, 1, 2):
         loads[i].wait()
     last = pl.ds(rows - GROUP, GROUP)
     tail_kv[...] = jnp.concatenate(
@@ -239,6 +233,12 @@
     ]
     tails[0].start()
     tails[1].start()
+
+    loads[3].wait()
+
+    @pl.loop(0, blocks)
+    def _(b):
+        send_f[lanes(b), :] = f_in[:, lanes(b)].T
 
     def own_rows(peer, h):
         return pl.ds(pl.multiple_of(h * (width // halves) + peer * GROUP, GROUP), GROUP)

time: 32.2 us -> 32.3 us (level)
  no operation moved by 1% of the time
where the time goes in v7:
time: 32.3 us; the launch traced here: 32.2 us
  Pallas kernels  30.7 us (95%)
  other arithmetic  0.83 us (3%)
  between operations  0.64 us (2%)
    pallas_call x1, Pallas kernels, shards(): pl.pallas_call(kernel, out_shape=(jax.ShapeDtypeStruct(block, F32), jax.S...  30.7 us
    convert_element_type x1, other arithmetic, shards(): normed = (stream_out.astype(F32) * scale[0][:, None] * gain[0]).astype(BF16)  0.83 us

profile of v7, /device:TPU:1, one launch (start us, length us, event | category | flops | bytes accessed | tf_op | source)
XLA Modules:
  0.0 32.2 jit_solution(13688425676207728773)
XLA Ops:
  0.6 30.7 %shard_map.113 = (f32[128,1024]{1,0:T(8,128)S(1)}, f32[1,128]{1,0:T(1,128)S(1)}, f32[1,1024]{1,0:T(1,128)S(1)}) custom-call(bf16[128,1024]{1,0:T(8,128)(2,1)} %queries.1, bf16[128,1024]{1,0:T(8,128)(2,1)} %keys.1, bf16[128,1024]{1,0:T(8,128)(2,1)} %values.1, bf16[128,1024]{1,0:T(8,128)(2,1)} %filters.1, bf16[3,7,1024]{2,1,0:T(8,128)(2,1)} %short_taps.1, ...), custom_call_target="tpu_custom_call" | custom-call | flops 2000000000 | bytes 2000000 | tf_op jit(solution)/shard_map/pallas_call | solution.py:427
  31.4 0.8 %multiply_convert_fusion = (bf16[128,1024]{1,0:T(8,128)(2,1)}, bf16[128,1024]{1,0:T(8,128)(2,1)}) fusion(f32[1024]{0:T(1024)S(1)} %bitcast.4, f32[128]{0:T(128)S(1)} %bitcast.5, f32[128,1024]{1,0:T(8,128)S(1)} %get-tuple-element.5), kind=kLoop, calls=%fused_computation | loop fusion | flops 655360 | bytes 1053184 | tf_op jit(solution)/shard_map/convert_element_type | solution.py:486

commit v8 on v4

--- a/solution.py
+++ b/solution.py
@@ -25,7 +25,7 @@
 )
 PLACE = {k1: i for i, k1 in enumerate(KEPT)}
 ROWS = len(KEPT) * GROUP
-CHUNK = 11 * GROUP
+CHUNK = 33 * GROUP
 
 
 STEPS = sorted(

time: 32.2 us -> 32.3 us (level)
  no operation moved by 1% of the time
where the time goes in v8:
time: 32.3 us; the launch traced here: 32.2 us
  Pallas kernels  30.7 us (95%)
  other arithmetic  0.83 us (3%)
  between operations  0.64 us (2%)
    pallas_call x1, Pallas kernels, shards(): pl.pallas_call(kernel, out_shape=(jax.ShapeDtypeStruct(block, F32), jax.S...  30.7 us
    convert_element_type x1, other arithmetic, shards(): normed = (stream_out.astype(F32) * scale[0][:, None] * gain[0]).astype(BF16)  0.83 us

profile of v8, /device:TPU:1, one launch (start us, length us, event | category | flops | bytes accessed | tf_op | source)
XLA Modules:
  0.0 32.2 jit_solution(10697786176216057230)
XLA Ops:
  0.6 30.7 %shard_map.113 = (f32[128,1024]{1,0:T(8,128)S(1)}, f32[1,128]{1,0:T(1,128)S(1)}, f32[1,1024]{1,0:T(1,128)S(1)}) custom-call(bf16[128,1024]{1,0:T(8,128)(2,1)} %queries.1, bf16[128,1024]{1,0:T(8,128)(2,1)} %keys.1, bf16[128,1024]{1,0:T(8,128)(2,1)} %values.1, bf16[128,1024]{1,0:T(8,128)(2,1)} %filters.1, bf16[3,7,1024]{2,1,0:T(8,128)(2,1)} %short_taps.1, ...), custom_call_target="tpu_custom_call" | custom-call | flops 2000000000 | bytes 2000000 | tf_op jit(solution)/shard_map/pallas_call | solution.py:427
  31.4 0.8 %multiply_convert_fusion = (bf16[128,1024]{1,0:T(8,128)(2,1)}, bf16[128,1024]{1,0:T(8,128)(2,1)}) fusion(f32[1024]{0:T(1024)S(1)} %bitcast.4, f32[128]{0:T(128)S(1)} %bitcast.5, f32[128,1024]{1,0:T(8,128)S(1)} %get-tuple-element.5), kind=kLoop, calls=%fused_computation | loop fusion | flops 655360 | bytes 1053184 | tf_op jit(solution)/shard_map/convert_element_type | solution.py:486
